TPU v7x, 32 devices: a whole 2x2x4 slice. The times are simulated.
32 devices in a mesh: groups: 2 (over y), row: 4 (over z), col: 4 (over x, core).
Axes of the slice: x: 2, y: 2, z: 4, core: 2. Of those that a mesh axis runs over, the one named last changes fastest.
Arguments:
- pair: bfloat16 [512, 256, 128], P(('groups', 'row'), 'col'), parts along dimension 0, may hold values from -6 to 6
- mask: int32 [512], P('groups'), parts along dimension 0, may hold values 0 or 1
- ln_gain: float32 [128], replicated, may hold values from 0.5 to 2
- ln_bias: float32 [128], replicated, may hold values from -3 to 3
- w_left: bfloat16 [128, 256], replicated, may hold values from -0.5 to 0.5
- w_right: bfloat16 [128, 256], replicated, may hold values from -0.5 to 0.5
- w_gate: bfloat16 [128, 128], replicated, may hold values from -0.5 to 0.5
- w_out: bfloat16 [128, 128], replicated, may hold values from -0.5 to 0.5
- out_gain: float32 [128], replicated, may hold values from 0.5 to 2
- out_bias: float32 [128], replicated, may hold values from -3 to 3
Outputs:
- update: bfloat16 [512, 256, 128], P(('groups', 'row'), 'col'), parts along dimension 0
There are 2 independent parts, one for each index of `groups`. A program takes and returns all parts, laid end to end along the dimension named above; an argument that names none is the same for every part. Nothing has to cross between parts.
Inputs may be any that keep to these rules, and one draw needn't show every extreme that they name: `mask`: 1 marks a valid token.
All inputs are finite; a program needn't handle non-finite values.
Results may differ from a plain program's by a relative error of at most 0.0059.
Values may be sent and summed in bfloat16 or wider, within the bound.
A program may use at most 64 MiB of HBM per device.

v0:
```python
import jax
import jax.numpy as jnp
from jax import lax
from jax.sharding import PartitionSpec as P


def layer_norm(values, scaling, shifting, reduce_axis):
    average = jnp.mean(values, axis=reduce_axis, keepdims=True)
    centered = values - average
    variance = jnp.mean(centered * centered, axis=reduce_axis, keepdims=True)
    return centered * lax.rsqrt(variance + 1e-05) * scaling + shifting


def body(pair, mask, ln_gain, ln_bias, w_left, w_right, w_gate, w_out, out_gain, out_bias):
    tile_rows, tile_cols, width = pair.shape
    hidden_width = w_out.shape[0]
    cells = tile_rows * tile_cols
    validity = mask.astype(jnp.float32)
    row_valid = lax.dynamic_slice_in_dim(validity, lax.axis_index("row") * tile_rows, tile_rows)
    col_valid = lax.dynamic_slice_in_dim(validity, lax.axis_index("col") * tile_cols, tile_cols)
    cell_mask = (row_valid[:, None] * col_valid[None, :]).reshape(1, cells)
    normed = layer_norm(pair.astype(jnp.float32), ln_gain, ln_bias, 2).astype(jnp.bfloat16)
    flattened = normed.reshape(cells, width)
    side_weights = jnp.concatenate([w_left, w_right], axis=1)
    joined = jnp.einsum("de,nd->en", side_weights, flattened, preferred_element_type=jnp.float32)
    joined = joined.reshape(2, 2, hidden_width, cells)
    left_right = (jax.nn.sigmoid(joined[:, 1]) * joined[:, 0] * cell_mask).astype(jnp.bfloat16)
    left_right = left_right.reshape(2, hidden_width, tile_rows, tile_cols)
    gate_values = jax.nn.sigmoid(jnp.dot(flattened, w_gate, preferred_element_type=jnp.float32))
    exchanged = lax.all_to_all(
        lax.all_to_all(left_right, "row", split_axis=1, concat_axis=2, tiled=True),
        "col",
        split_axis=1,
        concat_axis=3,
        tiled=True,
    )
    plane = jnp.einsum(
        "cik,cjk->cij", exchanged[0], exchanged[1], preferred_element_type=jnp.float32
    ).astype(jnp.bfloat16)
    combined = lax.all_to_all(
        lax.all_to_all(plane, "row", split_axis=1, concat_axis=0, tiled=True),
        "col",
        split_axis=2,
        concat_axis=0,
        tiled=True,
    )
    row_count = lax.axis_size("row")
    col_count = lax.axis_size("col")
    share_size = hidden_width // (row_count * col_count)

    def reorder(table):
        shaped = table.reshape((row_count, col_count, share_size) + table.shape[1:])
        return jnp.swapaxes(shaped, 0, 1).reshape(table.shape)

    gain_used = reorder(out_gain)
    bias_used = reorder(out_bias)
    weight_used = reorder(w_out)
    combined = combined.astype(jnp.float32).reshape(hidden_width, cells)
    normed_out = layer_norm(combined, gain_used[:, None], bias_used[:, None], 0).astype(
        jnp.bfloat16
    )
    projected = jnp.einsum("hn,hc->nc", normed_out, weight_used, preferred_element_type=jnp.float32)
    return (gate_values * projected).reshape(tile_rows, tile_cols, width).astype(jnp.bfloat16)


def solution(mesh):
    return jax.shard_map(
        body,
        mesh=mesh,
        in_specs=(
            P(("groups", "row"), "col", None),
            P("groups"),
            P(),
            P(),
            P(),
            P(),
            P(),
            P(),
            P(),
            P(),
        ),
        out_specs=P(("groups", "row"), "col", None),
        check_vma=False,
    )
```

profile of v0, /device:TPU:0, one launch (start us, length us, event | category | flops | bytes accessed | tf_op | source)
XLA Modules:
  0.0 202.3 jit_solution(18439636473183912386)
XLA Ops:
  0.8 1.8 convert_reduce_fusion
  2.7 2.3 %fusion.9 = f32[64,64]{1,0:T(8,128)S(1)} fusion(bf16[64,64,128]{2,1,0:T(8,128)(2,1)} %param.10, f32[64,64]{1,0:T(8,128)S(1)} %broadcast_multiply_fusion.2), kind=kLoop, calls=%fused_computation.20 | loop fusion | flops 2093056 | bytes 1081344 | tf_op jit(solution)/shard_map/reduce_sum | solution.py:10
  5.2 1.3 fusion.12
  8.7 3.0 %slice_multiply_fusion = f32[2,1,128,4096]{3,2,1,0:T(8,128)} fusion(f32[2,2,128,4096]{3,2,1,0:T(8,128)S(1)} %fusion.15), kind=kLoop, calls=%fused_computation.6 | loop fusion | flops 4194304 | bytes 12582912 | tf_op jit(solution)/shard_map/mul | solution.py:27
  11.8 5.6 %copy.58 = f32[2,1,128,4096]{2,3,0,1:T(8,128)} copy(f32[2,1,128,4096]{3,2,1,0:T(8,128)} %slice_multiply_fusion) | data formatting | bytes 8388608 | tf_op jit(solution)/shard_map/mul | solution.py:27
  17.5 2.7 %multiply_convert_fusion = bf16[2,128,64,64]{1,3,2,0:T(8,128)(2,1)S(1)} fusion(f32[2,128,64,64]{1,3,2,0:T(8,128)} %bitcast.54, f32[64,64]{1,0:T(8,128)S(1)} %broadcast_multiply_fusion), kind=kLoop, calls=%fused_computation.15 | loop fusion | flops 2097152 | bytes 6307840 | tf_op jit(solution)/shard_map/convert_element_type | solution.py:27
  20.2 6.5 %copy.59 = bf16[2,128,64,64]{3,2,0,1:T(8,128)(2,1)} copy(bf16[2,128,64,64]{1,3,2,0:T(8,128)(2,1)S(1)} %multiply_convert_fusion) | data formatting | bytes 4194304 | tf_op jit(solution)/shard_map/convert_element_type | solution.py:27
  26.7 4.9 %reshape.120 = bf16[4,2,131072]{2,1,0:T(2,128)(2,1)S(1)} reshape(bf16[128,2,64,64]{3,2,1,0:T(8,128)(2,1)} %bitcast.53) | data formatting | bytes 4194304
  31.6 54.4 %all_to_all.60 = bf16[4,2,131072]{2,1,0:T(2,128)(2,1)} all-to-all(bf16[4,2,131072]{2,1,0:T(2,128)(2,1)S(1)} %reshape.120), channel_id=1, replica_groups=mesh['groups'=2,'row'=4,'col'=4] {'row'}, dimensions={0} | all-to-all | bytes 4194304 | tf_op jit(solution)/shard_map/all_to_all | solution.py:31
  86.0 5.8 %reshape.121 = bf16[128,2,64,64]{3,2,1,0:T(8,128)(2,1)} reshape(bf16[4,2,131072]{2,1,0:T(2,128)(2,1)} %all_to_all.60) | data formatting | bytes 4194304
  91.9 7.5 %copy.80 = bf16[2,32,4,64,64]{3,2,4,0,1:T(4,128)(2,1)} copy(bf16[2,32,4,64,64]{4,3,0,1,2:T(8,128)(2,1)} %bitcast.55) | data formatting | bytes 4194304 | tf_op jit(solution)/shard_map/all_to_all | solution.py:31
  99.3 6.0 %reshape.119 = bf16[2,32,256,64]{2,3,0,1:T(8,128)(2,1)S(1)} reshape(bf16[2,32,4,64,64]{3,2,4,0,1:T(4,128)(2,1)} %copy.80) | data formatting | bytes 4194304 | tf_op jit(solution)/shard_map/all_to_all | solution.py:31
  105.3 28.3 %all_to_all.61 = bf16[2,32,256,64]{2,3,0,1:T(8,128)(2,1)S(1)} all-to-all(bf16[2,32,256,64]{2,3,0,1:T(8,128)(2,1)S(1)} %reshape.119), channel_id=1, replica_groups=mesh['groups'=2,'row'=4,'col'=4] {'col'}, dimensions={1} | all-to-all | bytes 4194304 | tf_op jit(solution)/shard_map/all_to_all | solution.py:30
  135.4 28.1 %all_to_all.62 = bf16[8,256,256]{2,0,1:T(8,128)(2,1)S(1)} all-to-all(bf16[8,256,256]{2,0,1:T(8,128)(2,1)S(1)} %copy.68), channel_id=1, replica_groups=mesh['groups'=2,'row'=4,'col'=4] {'row'}, dimensions={1} | all-to-all | bytes 2097152 | tf_op jit(solution)/shard_map/all_to_all | solution.py:41
  163.7 3.1 %copy.71 = bf16[32,64,256]{1,0,2:T(8,128)(2,1)S(1)} copy(bf16[32,64,256]{2,1,0:T(8,128)(2,1)S(1)} %bitcast.61) | data formatting | bytes 2097152 | tf_op jit(solution)/shard_map/all_to_all | solution.py:41
  166.8 2.7 %reshape.122 = bf16[4,2,65536]{2,1,0:T(2,128)(2,1)} reshape(bf16[256,32,64]{2,1,0:T(8,128)(2,1)S(1)} %bitcast.57) | data formatting | bytes 2097152
  169.5 3.6 %all-to-all-start.3 = ((bf16[4,2,65536]{2,1,0:T(2,128)(2,1)}), bf16[4,2,65536]{2,1,0:T(2,128)(2,1)S(1)}, u32[]{:S(2)}, u32[]{:S(2)}) async-start(bf16[4,2,65536]{2,1,0:T(2,128)(2,1)} %reshape.122), calls=%async_computation.3 | async-start | bytes 2097152 | tf_op jit(solution)/shard_map/all_to_all | solution.py:40
  173.6 2.0 %fusion.2 = f32[4096,128]{1,0:T(8,128)} fusion(bf16[4096,128]{1,0:T(8,128)(2,1)S(1)} %bitcast.63, bf16[128,128]{1,0:T(8,128)(2,1)S(1)} %copy-done), kind=kOutput, calls=%fused_computation.4 | convolution fusion | flops 135790592 | bytes 3178496 | tf_op jit(solution)/shard_map/dot_general | solution.py:29
  175.6 12.0 %all-to-all-done.3 = bf16[4,2,65536]{2,1,0:T(2,128)(2,1)S(1)} async-done(((bf16[4,2,65536]{2,1,0:T(2,128)(2,1)}), bf16[4,2,65536]{2,1,0:T(2,128)(2,1)S(1)}, u32[]{:S(2)}, u32[]{:S(2)}) %all-to-all-start.3) | async-done | bytes 1048608 | tf_op jit(solution)/shard_map/all_to_all | solution.py:40
  187.5 1.4 reshape.123
  189.0 3.7 %copy.72 = f32[32,64,4,64]{3,1,0,2:T(8,128)} copy(bf16[32,64,4,64]{1,0,3,2:T(8,128)(2,1)S(1)} %bitcast.56) | data formatting | bytes 3145728 | tf_op jit(solution)/shard_map/convert_element_type | solution.py:58
  192.7 2.7 %bitcast_reduce_fusion = f32[64,64]{1,0:T(8,128)S(1)} fusion(f32[32,64,4,64]{3,1,0,2:T(8,128)} %copy.72), kind=kLoop, calls=%fused_computation.12 | loop fusion | flops 520192 | bytes 2113536 | tf_op jit(solution)/shard_map/reduce_sum | solution.py:8
  197.6 1.7 convert_element_type.50
  199.3 3.0 %fusion.3 = bf16[4096,128]{1,0:T(8,128)(2,1)} fusion(f32[4096,128]{1,0:T(8,128)} %fusion.2, bf16[128,4096]{1,0:T(8,128)(2,1)S(1)} %convert_element_type.50, bf16[128,128]{1,0:T(8,128)(2,1)S(1)} %bitcast.66), kind=kOutput, calls=%fused_computation.5 | convolution fusion | flops 135266304 | bytes 4227072 | tf_op jit(solution)/shard_map/hn,hc->nc/dot_general | solution.py:62
  (50 shorter events, 7.9 us)
Async XLA Ops:
  0.0 173.5 %copy-start = (bf16[128,128]{1,0:T(8,128)(2,1)S(1)}, bf16[128,128]{1,0:T(8,128)(2,1)}, u32[]{:S(2)}) copy-start(bf16[128,128]{1,0:T(8,128)(2,1)} %param.16) | copy-start | bytes 98308
  0.0 5.2 %copy-start.2 = (bf16[64,64,128]{2,1,0:T(8,128)(2,1)S(1)}, bf16[64,64,128]{2,1,0:T(8,128)(2,1)}, u32[]{:S(2)}) copy-start(bf16[64,64,128]{2,1,0:T(8,128)(2,1)} %param.10) | copy-start | bytes 3145732
  0.0 5.0 %copy-start.6 = (bf16[128,256]{1,0:T(8,128)(2,1)S(1)}, bf16[128,256]{1,0:T(8,128)(2,1)}, u32[]{:S(2)}) copy-start(bf16[128,256]{1,0:T(8,128)(2,1)} %param.14) | copy-start | bytes 196612
  0.0 5.0 %copy-start.5 = (bf16[128,256]{1,0:T(8,128)(2,1)S(1)}, bf16[128,256]{1,0:T(8,128)(2,1)}, u32[]{:S(2)}) copy-start(bf16[128,256]{1,0:T(8,128)(2,1)} %param.15) | copy-start | bytes 196612
  0.0 5.2 %copy-start.11 = (f32[128]{0:T(128)S(1)}, f32[128]{0:T(128)}, u32[]{:S(2)}) copy-start(f32[128]{0:T(128)} %param.12) | copy-start | bytes 1540
  0.0 5.2 %copy-start.10 = (f32[128]{0:T(128)S(1)}, f32[128]{0:T(128)}, u32[]{:S(2)}) copy-start(f32[128]{0:T(128)} %param.13) | copy-start | bytes 1540
  6.5 1.0 copy-start.3
  166.8 6.3 %copy-start.8 = (f32[128]{0:T(128)S(1)}, f32[128]{0:T(128)}, u32[]{:S(2)}) copy-start(f32[128]{0:T(128)} %param.19) | copy-start | bytes 1540
  166.8 6.5 %copy-start.9 = (f32[128]{0:T(128)S(1)}, f32[128]{0:T(128)}, u32[]{:S(2)}) copy-start(f32[128]{0:T(128)} %param.18) | copy-start | bytes 1540
  166.8 6.7 %copy-start.7 = (bf16[128,128]{1,0:T(8,128)(2,1)S(1)}, bf16[128,128]{1,0:T(8,128)(2,1)}, u32[]{:S(2)}) copy-start(bf16[128,128]{1,0:T(8,128)(2,1)} %param.17) | copy-start | bytes 98308
  169.5 4.1 %copy-start.4 = (bf16[64,64,128]{2,1,0:T(8,128)(2,1)S(1)}, bf16[64,64,128]{2,1,0:T(8,128)(2,1)}, u32[]{:S(2)}) copy-start(bf16[64,64,128]{2,1,0:T(8,128)(2,1)} %copy-done.3) | copy-start | bytes 3145732
  169.5 18.1 %all-to-all-start.3 = ((bf16[4,2,65536]{2,1,0:T(2,128)(2,1)}), bf16[4,2,65536]{2,1,0:T(2,128)(2,1)S(1)}, u32[]{:S(2)}, u32[]{:S(2)}) async-start(bf16[4,2,65536]{2,1,0:T(2,128)(2,1)} %reshape.122), calls=%async_computation.3 | async-start | bytes 2097152 | tf_op jit(solution)/shard_map/all_to_all | solution.py:40
  192.7 3.4 %copy-start.1 = (f32[32,64,4,64]{3,1,0,2:T(8,128)S(1)}, f32[32,64,4,64]{3,1,0,2:T(8,128)}, u32[]{:S(2)}) copy-start(f32[32,64,4,64]{3,1,0,2:T(8,128)} %copy.72) | copy-start | bytes 6291460
where the time goes:
time: 203 us; the launch traced here: 202 us
  blocking collectives  111 us (55%)
  local copies, waits for them, and re-layouts  52.7 us (26%)
  other arithmetic  16.1 us (8%)
  waiting for transfers between devices  12 us (6%)
  matrix products  6.83 us (3%)
  starting transfers between devices  3.65 us (2%)
    all_to_all x1, blocking collectives, body(): lax.all_to_all(left_right, 'row', split_axis=1, concat_axis=2, tiled=True)  54.4 us
    all_to_all x1, blocking collectives, body(): lax.all_to_all(lax.all_to_all(left_right, 'row', split_axis=1, concat_axi...  28.3 us
    all_to_all x1, blocking collectives, body(): lax.all_to_all(plane, 'row', split_axis=1, concat_axis=0, tiled=True)  28.1 us
    unnamed x28, local copies, waits for them, and re-layouts  16.6 us
    all_to_all x2, local copies, waits for them, and re-layouts, body(): lax.all_to_all(left_right, 'row', split_axis=1, concat_axis=2, tiled=True)  13.4 us
    all_to_all x1, waiting for transfers between devices, body(): lax.all_to_all(lax.all_to_all(plane, 'row', split_axis=1, concat_axis=0,...  12 us
    convert_element_type x1, local copies, waits for them, and re-layouts, body(): (jax.nn.sigmoid(joined[:, 1]) * joined[:, 0] * cell_mask).astype(jnp.bflo...  6.48 us
    mul x1, local copies, waits for them, and re-layouts, body(): jax.nn.sigmoid(joined[:, 1]) * joined[:, 0] * cell_mask  5.62 us
  transfers between devices with their start and end apart: 1, of which 1 were waited for; matrix products, arithmetic and copies ran while one was open for 1% of the time, Pallas kernels for 0%

commit v1 on v0

v1 whole, which is shorter than its diff:
```python
import functools

import jax
import jax.numpy as jnp
from jax import lax
from jax.experimental import pallas as pl
from jax.experimental.pallas import tpu as pltpu
from jax.sharding import PartitionSpec as P

MESH = pl.DeviceIdType.MESH
NT = (((1,), (1,)), ((), ()))
TN = (((0,), (0,)), ((), ()))
LIMIT = 56 * 1024 * 1024


def halves(a, b, half):
    low = jnp.concatenate([a[:, :half], b[:, :half]], axis=1)
    high = jnp.concatenate([a[:, half:], b[:, half:]], axis=1)
    return low, high


def project(steps, pair_ref, mask_ref, gain_ref, bias_ref, side_ref, wg_ref, left_ref, right_ref, gate_ref, scratch):
    folds, depth, cols, width = pair_ref.shape
    lanes = folds * cols
    hidden = side_ref.shape[0] // 4
    gain, bias = gain_ref[...], bias_ref[...]

    def step(n, carry):
        t0 = n * steps
        rows = [pair_ref[p, t0 + s] for s in range(steps) for p in range(folds)]
        x = jnp.concatenate(rows, axis=0).astype(jnp.float32)
        x = x - jnp.mean(x, axis=1, keepdims=True)
        x = x * lax.rsqrt(jnp.mean(x * x, axis=1, keepdims=True) + 1e-05) * gain + bias
        x = x.astype(jnp.bfloat16)
        gate = jax.nn.sigmoid(jnp.dot(x, wg_ref[...], preferred_element_type=jnp.float32))
        for s in range(steps):
            gate_ref[t0 + s] = gate[s * lanes : (s + 1) * lanes]
        for side in range(2):
            weights = side_ref[side * 2 * hidden : (side + 1) * 2 * hidden]
            joined = lax.dot_general(weights, x, NT, preferred_element_type=jnp.float32)
            for s in range(steps):
                part = joined[:, s * lanes : (s + 1) * lanes]
                value = jax.nn.sigmoid(part[hidden:]) * part[:hidden] * mask_ref[pl.ds(t0 + s, 1), :]
                scratch[side, pl.ds(t0 + s, hidden, stride=depth), :] = value
        return carry

    lax.fori_loop(0, depth // steps, step, 0)
    for side, ref in enumerate((left_ref, right_ref)):
        block = ref.shape[2]

        def cast(n, carry, side=side, ref=ref, block=block):
            at = pl.multiple_of(n * block, block)
            ref[n // ref.shape[1], n % ref.shape[1]] = scratch[side, pl.ds(at, block), :].astype(jnp.bfloat16)
            return carry

        lax.fori_loop(0, ref.shape[0] * ref.shape[1], cast, 0)


def exchange(plan, left_ref, right_ref, out_ref, lbuf, rbuf, sbuf, lsend, rsend, ssend, lrecv, rrecv, crecv):
    nrow, ncol, nh, nu, depth = plan
    per_half = nrow // nh
    me_row, me_col = lax.axis_index("row"), lax.axis_index("col")
    my_half = me_row // per_half
    rows = left_ref.shape[2]
    units = rows // depth

    def owner(h, u):
        if nh == 1:
            return u
        return jnp.where(u == 0, h * (nrow - 1), h + per_half - 1)

    def slot(u):
        return u * 0 if nh == 1 else jnp.maximum(u - 1, 0)

    if nh == 1:
        first, count = me_row, 1
    else:
        inner = jnp.logical_and(me_row > 0, me_row < nrow - 1)
        first, count = jnp.where(inner, 1, 0), jnp.where(inner, nu - 1, 1)

    barrier = pltpu.get_barrier_semaphore()
    others = nrow * ncol - 1

    def greet(n, carry):
        at = lax.rem(me_row * ncol + me_col + 1 + n, nrow * ncol)
        pl.semaphore_signal(barrier, 1, device_id={"row": at // ncol, "col": at % ncol}, device_id_type=MESH)
        return carry

    lax.fori_loop(0, others, greet, 0)
    pl.semaphore_wait(barrier, others)

    def move(row, col, src, dst, send, recv, begin):
        same = jnp.logical_and(row == me_row, col == me_col)
        remote = pltpu.make_async_remote_copy(
            src_ref=src, dst_ref=dst, send_sem=send, recv_sem=recv,
            device_id={"row": row, "col": col}, device_id_type=MESH,
        )

        @pl.when(jnp.logical_not(same))
        def _():
            if begin:
                remote.start()
            else:
                remote.wait_send()

        if begin:
            @pl.when(same)
            def _():
                pltpu.make_async_copy(src, dst, recv).start()

    def spread(begin):
        def body(n, carry):
            u = n // ncol
            col = lax.rem(me_col + n, ncol)
            m = slot(u)
            move(owner(my_half, u), col, left_ref.at[col, u], lbuf.at[m, me_row % per_half, me_col],
                 lsend.at[n], lrecv.at[m], begin)
            for d in range(nh):
                h = lax.rem(my_half + 1 + d, nh)
                move(owner(h, u), col, right_ref.at[col, u], rbuf.at[m, me_row, me_col],
                     rsend.at[n * nh + d], rrecv.at[m], begin)
            return carry

        lax.fori_loop(0, nu * ncol, body, 0)

    spread(True)

    def give(m, begin):
        def body(n, carry):
            b, col = n // ncol, lax.rem(me_col + n, ncol)
            move(my_half * per_half + b, col, sbuf.at[m, b, col], out_ref.at[me_col, first + m],
                 ssend.at[m * per_half * ncol + n], crecv, begin)
            return carry

        lax.fori_loop(0, per_half * ncol, body, 0)

    half = 64

    def gather(buf, m, blocks, at):
        strips = []
        for b in range(blocks):
            low, high = [], []
            for q in range(0, ncol, 2):
                lo, hi = halves(buf[m, b, q, pl.ds(at, depth), :], buf[m, b, q + 1, pl.ds(at, depth), :], half)
                low.append(lo)
                high.append(hi)
            strips += [jnp.concatenate(low, axis=1), jnp.concatenate(high, axis=1)]
        return jnp.concatenate(strips, axis=0)

    def work(m, carry):
        pltpu.make_async_copy(lbuf.at[m], lbuf.at[m], lrecv.at[m]).wait()
        pltpu.make_async_copy(rbuf.at[m], rbuf.at[m], rrecv.at[m]).wait()

        def channel(c, carry):
            at = pl.multiple_of(c * depth, depth)
            a = gather(lbuf, m, per_half, at)
            b = gather(rbuf, m, nrow, at)
            d = lax.dot_general(a, b, NT, preferred_element_type=jnp.float32).astype(jnp.bfloat16)
            for blk in range(per_half):
                top = d[blk * 2 * depth : blk * 2 * depth + depth]
                low = d[blk * 2 * depth + depth : (blk + 1) * 2 * depth]
                for q in range(0, ncol, 2):
                    span = slice(q * half, (q + 2) * half)
                    lo, hi = halves(top[:, span], low[:, span], half)
                    sbuf[m, blk, q, pl.ds(at, depth), :] = lo
                    sbuf[m, blk, q + 1, pl.ds(at, depth), :] = hi
            return carry

        lax.fori_loop(0, units, channel, 0)
        give(m, True)
        return carry

    lax.fori_loop(0, count, work, 0)
    pltpu.make_async_copy(out_ref, out_ref, crecv).wait()
    spread(False)

    def finish(m, carry):
        give(m, False)
        return carry

    lax.fori_loop(0, count, finish, 0)


def output(plane_ref, gate_ref, gain_ref, bias_ref, wo_ref, out_ref, scratch):
    folds, depth, cols, width = out_ref.shape
    hidden = wo_ref.shape[0]
    block = 512

    def cast(n, carry):
        at = pl.multiple_of(n * block, block)
        scratch[pl.ds(at, block), :] = plane_ref[pl.ds(at, block), :].astype(jnp.float32)
        return carry

    lax.fori_loop(0, hidden * depth // block, cast, 0)

    def step(t, carry):
        x = scratch[pl.ds(t, hidden, stride=depth), :]
        x = x - jnp.mean(x, axis=0, keepdims=True)
        x = x * lax.rsqrt(jnp.mean(x * x, axis=0, keepdims=True) + 1e-05) * gain_ref[...] + bias_ref[...]
        y = lax.dot_general(x.astype(jnp.bfloat16), wo_ref[...], TN, preferred_element_type=jnp.float32)
        y = (y * gate_ref[t]).astype(jnp.bfloat16)
        for p in range(folds):
            out_ref[p, t] = y[p * cols : (p + 1) * cols]
        return carry

    lax.fori_loop(0, depth, step, 0, unroll=2)


def body(nrow, ncol, pair, mask, ln_gain, ln_bias, w_left, w_right, w_gate, w_out, out_gain, out_bias):
    tile_rows, tile_cols, width = pair.shape
    hidden = w_out.shape[0]
    lanes = 128
    folds = lanes // tile_cols
    depth = tile_rows // folds
    nh, nu = (2, 4) if nrow == 4 else (1, nrow)
    slots = nu - 1 if nh == 2 else 1
    per_half = nrow // nh
    rows = hidden // (ncol * nu) * depth
    validity = mask.astype(jnp.float32)
    row_valid = lax.dynamic_slice_in_dim(validity, lax.axis_index("row") * tile_rows, tile_rows)
    col_valid = lax.dynamic_slice_in_dim(validity, lax.axis_index("col") * tile_cols, tile_cols)
    cells = row_valid.reshape(folds, depth).T[:, :, None] * col_valid[None, None, :]
    cells = cells.reshape(depth, lanes)
    side_weights = jnp.concatenate([w_left, w_right], axis=1).T
    vmem = pl.BlockSpec(memory_space=pltpu.VMEM)
    anywhere = pl.BlockSpec(memory_space=pl.ANY)
    packed = jax.ShapeDtypeStruct((ncol, nu, rows, lanes), jnp.bfloat16)
    left, right, gate = pl.pallas_call(
        functools.partial(project, 4),
        out_shape=(packed, packed, jax.ShapeDtypeStruct((depth, lanes, width), jnp.float32)),
        in_specs=[vmem] * 6,
        out_specs=(vmem,) * 3,
        scratch_shapes=[pltpu.VMEM((2, hidden * depth, lanes), jnp.float32)],
        compiler_params=pltpu.CompilerParams(vmem_limit_bytes=LIMIT),
    )(
        pair.reshape(folds, depth, tile_cols, width), cells,
        ln_gain.reshape(1, width), ln_bias.reshape(1, width), side_weights, w_gate,
    )
    plane = pl.pallas_call(
        functools.partial(exchange, (nrow, ncol, nh, nu, depth)),
        out_shape=packed,
        in_specs=[anywhere] * 2,
        out_specs=anywhere,
        scratch_shapes=[
            pltpu.VMEM((slots, per_half, ncol, rows, lanes), jnp.bfloat16),
            pltpu.VMEM((slots, nrow, ncol, rows, lanes), jnp.bfloat16),
            pltpu.VMEM((slots, per_half, ncol, rows, lanes), jnp.bfloat16),
            pltpu.SemaphoreType.DMA((nu * ncol,)),
            pltpu.SemaphoreType.DMA((nu * ncol * nh,)),
            pltpu.SemaphoreType.DMA((slots * per_half * ncol,)),
            pltpu.SemaphoreType.DMA((slots,)),
            pltpu.SemaphoreType.DMA((slots,)),
            pltpu.SemaphoreType.DMA,
        ],
        compiler_params=pltpu.CompilerParams(
            collective_id=0, has_side_effects=True, vmem_limit_bytes=LIMIT
        ),
    )(left, right)
    out = pl.pallas_call(
        output,
        out_shape=jax.ShapeDtypeStruct((folds, depth, tile_cols, width), jnp.bfloat16),
        in_specs=[vmem] * 5,
        out_specs=vmem,
        scratch_shapes=[pltpu.VMEM((hidden * depth, lanes), jnp.float32)],
        compiler_params=pltpu.CompilerParams(vmem_limit_bytes=LIMIT),
    )(
        plane.reshape(hidden * depth, lanes), gate,
        jnp.broadcast_to(out_gain[:, None], (hidden, lanes)),
        jnp.broadcast_to(out_bias[:, None], (hidden, lanes)), w_out,
    )
    return out.reshape(tile_rows, tile_cols, width)


def solution(mesh):
    return jax.shard_map(
        functools.partial(body, mesh.shape["row"], mesh.shape["col"]),
        mesh=mesh,
        in_specs=(P(("groups", "row"), "col", None), P("groups"), P(), P(), P(), P(), P(), P(), P(), P()),
        out_specs=P(("groups", "row"), "col", None),
        check_vma=False,
    )
```

time: 203 us -> 101 us (0.50)
  blocking collectives: 111 us -> 0 us
  Pallas kernels: 0 us -> 94.7 us
  local copies, waits for them, and re-layouts: 52.7 us -> 3.82 us
  other arithmetic: 16.1 us -> 1.94 us
  waiting for transfers between devices: 12 us -> 0 us
  matrix products: 6.83 us -> 0 us
  starting transfers between devices: 3.65 us -> 0 us
    all_to_all x3 -> x0, blocking collectives: 111 us -> none  [the longest x1 54.4 us: body(): lax.all_to_all(left_right, 'row', split_axis=1, concat_axis=2, tiled=True)]
    pallas_call x0 -> x3, Pallas kernels: none -> 94.7 us  [the longest x1 76.1 us: body(): pl.pallas_call(functools.partial(exchange, (nrow, ncol, nh, nu, depth)),...]
    all_to_all x5 -> x0, local copies, waits for them, and re-layouts: 17 us -> none  [the longest x2 13.4 us: body(): lax.all_to_all(left_right, 'row', split_axis=1, concat_axis=2, tiled=True)]
    unnamed x28 -> x6, local copies, waits for them, and re-layouts: 16.6 us -> 1.91 us
    convert_element_type x4 -> x0, local copies, waits for them, and re-layouts: 12.5 us -> none  [the longest x1 6.48 us: body(): (jax.nn.sigmoid(joined[:, 1]) * joined[:, 0] * cell_mask).astype(jnp.bflo...]
    all_to_all x1 -> x0, waiting for transfers between devices: 12 us -> none  [body(): lax.all_to_all(lax.all_to_all(plane, 'row', split_axis=1, concat_axis=0,...]
    reduce_sum x4 -> x0, other arithmetic: 7.46 us -> none  [the longest x2 4.52 us: layer_norm(): average = jnp.mean(values, axis=reduce_axis, keepdims=True)]
    dot_general x4 -> x0, matrix products: 6.83 us -> none  [the longest x1 3.05 us: body(): jnp.einsum('hn,hc->nc', normed_out, weight_used, preferred_element_type=j...]
  transfers between devices with their start and end apart: 1 -> 0, of which waited for: 1 -> 0; matrix products, arithmetic and copies ran while one was open for 1% -> 0% of each run, Pallas kernels for 0% -> 0%
where the time goes in v1:
time: 101 us; the launch traced here: 100 us
  Pallas kernels  94.7 us (94%)
  local copies, waits for them, and re-layouts  3.82 us (4%)
  other arithmetic  1.94 us (2%)
    pallas_call x1, Pallas kernels, body(): pl.pallas_call(functools.partial(exchange, (nrow, ncol, nh, nu, depth)),...  76.1 us
    pallas_call x1, Pallas kernels, body(): pl.pallas_call(functools.partial(project, 4), out_shape=(packed, packed,...  9.84 us
    pallas_call x1, Pallas kernels, body(): pl.pallas_call(output, out_shape=jax.ShapeDtypeStruct((folds, depth, tile...  8.68 us

profile of v1, /device:TPU:0, one launch (start us, length us, event | category | flops | bytes accessed | tf_op | source)
XLA Modules:
  0.0 100.5 jit_solution(5036114457221692397)
XLA Ops:
  0.0 0.7 convert_element_type.3
  0.7 0.1 fusion
  0.8 0.1 reshape.26
  0.8 0.1 copy.11
  0.9 0.1 mul.27
  1.0 0.1 mul.28
  1.1 0.1 mul.31
  1.2 0.6 broadcast_multiply_fusion.mask_ref
  1.8 0.9 copy.12
  2.8 1.0 copy.13
  3.7 0.7 maximum_bitcast_fusion.side_ref
  4.4 0.0 copy-start
  4.4 0.0 copy-start.1
  4.4 9.8 %shard_map.100 = (bf16[4,4,256,128]{3,2,1,0:T(8,128)(2,1)}, bf16[4,4,256,128]{3,2,1,0:T(8,128)(2,1)}, f32[32,128,128]{2,1,0:T(8,128)}) custom-call(bf16[2,32,64,128]{3,2,1,0:T(8,128)(2,1)} %bitcast.9, f32[32,128]{1,0:T(8,128)} %broadcast_multiply_fusion.mask_ref, f32[1,128]{1,0:T(1,128)} %bitcast.11, f32[1,128]{1,0:T(1,128)} %bitcast.12, ...), custom_call_target="tpu_custom_call" | custom-call | tf_op jit(solution)/shard_map/pallas_call | solution.py:228
  14.2 76.1 %shard_map.101 = bf16[4,4,256,128]{3,2,1,0:T(8,128)(2,1)} custom-call(bf16[4,4,256,128]{3,2,1,0:T(8,128)(2,1)} %get-tuple-element.8.left_ref, bf16[4,4,256,128]{3,2,1,0:T(8,128)(2,1)} %get-tuple-element.9.right_ref), custom_call_target="tpu_custom_call" | custom-call | tf_op jit(solution)/shard_map/pallas_call | solution.py:239
  90.4 0.0 copy-done
  90.4 0.7 broadcast_in_dim.4.gain_ref
  91.1 0.0 copy-done.1
  91.1 0.7 broadcast_in_dim.5.bias_ref
  91.8 8.7 %shard_map.102 = bf16[2,32,64,128]{3,2,1,0:T(8,128)(2,1)} custom-call(bf16[4096,128]{1,0:T(8,128)(2,1)} %bitcast.8, f32[32,128,128]{2,1,0:T(8,128)} %get-tuple-element.10.gate_ref, f32[128,128]{1,0:T(8,128)} %broadcast_in_dim.4.gain_ref, f32[128,128]{1,0:T(8,128)} %broadcast_in_dim.5.bias_ref, bf16[128,128]{1,0:T(8,128)(2,1)} %wo_ref.1), custom_call_target="tpu_custom_call" | custom-call | tf_op jit(solution)/shard_map/pallas_call | solution.py:259
  (1 shorter events, 0.0 us)
Async XLA Ops:
  4.4 86.0 %copy-start = (f32[128]{0:T(128)S(1)}, f32[128]{0:T(128)}, u32[]{:S(2)}) copy-start(f32[128]{0:T(128)} %param.18) | copy-start | bytes 1540
  4.4 86.7 %copy-start.1 = (f32[128]{0:T(128)S(1)}, f32[128]{0:T(128)}, u32[]{:S(2)}) copy-start(f32[128]{0:T(128)} %param.19) | copy-start | bytes 1540

commit v2 on v1

--- a/solution.py
+++ b/solution.py
@@ -19,11 +19,22 @@
     return low, high
 
 
-def project(steps, pair_ref, mask_ref, gain_ref, bias_ref, side_ref, wg_ref, left_ref, right_ref, gate_ref, scratch):
+def project(steps, pair_ref, flag_ref, cols_ref, gain_ref, bias_ref, wl_ref, wr_ref, wg_ref, left_ref, right_ref, gate_ref, scratch):
     folds, depth, cols, width = pair_ref.shape
     lanes = folds * cols
-    hidden = side_ref.shape[0] // 4
+    hidden = wl_ref.shape[1] // 2
     gain, bias = gain_ref[...], bias_ref[...]
+    sides = [ref[...].astype(jnp.float32).T.astype(jnp.bfloat16) for ref in (wl_ref, wr_ref)]
+    first_row = lax.axis_index("row") * (folds * depth)
+    col_valid = cols_ref[pl.ds(lax.axis_index("col"), 1), :].astype(jnp.float32)
+    col_valid = jnp.concatenate([col_valid] * folds, axis=1)
+    fold = lax.broadcasted_iota(jnp.int32, (1, lanes), 1) // cols
+
+    def valid(t):
+        flags = flag_ref[first_row + t]
+        for p in range(1, folds):
+            flags = jnp.where(fold == p, flag_ref[first_row + p * depth + t], flags)
+        return col_valid * flags.astype(jnp.float32)
 
     def step(n, carry):
         t0 = n * steps
@@ -35,12 +46,12 @@
         gate = jax.nn.sigmoid(jnp.dot(x, wg_ref[...], preferred_element_type=jnp.float32))
         for s in range(steps):
             gate_ref[t0 + s] = gate[s * lanes : (s + 1) * lanes]
+        valids = [valid(t0 + s) for s in range(steps)]
         for side in range(2):
-            weights = side_ref[side * 2 * hidden : (side + 1) * 2 * hidden]
-            joined = lax.dot_general(weights, x, NT, preferred_element_type=jnp.float32)
+            joined = lax.dot_general(sides[side], x, NT, preferred_element_type=jnp.float32)
             for s in range(steps):
                 part = joined[:, s * lanes : (s + 1) * lanes]
-                value = jax.nn.sigmoid(part[hidden:]) * part[:hidden] * mask_ref[pl.ds(t0 + s, 1), :]
+                value = jax.nn.sigmoid(part[hidden:]) * part[:hidden] * valids[s]
                 scratch[side, pl.ds(t0 + s, hidden, stride=depth), :] = value
         return carry
 
@@ -56,13 +67,14 @@
         lax.fori_loop(0, ref.shape[0] * ref.shape[1], cast, 0)
 
 
-def exchange(plan, left_ref, right_ref, out_ref, lbuf, rbuf, sbuf, lsend, rsend, ssend, lrecv, rrecv, crecv):
+def exchange(plan, left_ref, right_ref, out_ref, lbuf, rbuf, sbuf, lsend, rsend, ssend, lrecv, rrecv, crecv, relays):
     nrow, ncol, nh, nu, depth = plan
     per_half = nrow // nh
     me_row, me_col = lax.axis_index("row"), lax.axis_index("col")
     my_half = me_row // per_half
     rows = left_ref.shape[2]
     units = rows // depth
+    slots = lbuf.shape[0]
 
     def owner(h, u):
         if nh == 1:
@@ -89,14 +101,14 @@
     lax.fori_loop(0, others, greet, 0)
     pl.semaphore_wait(barrier, others)
 
-    def move(row, col, src, dst, send, recv, begin):
+    def move(row, col, src, dst, send, recv, begin, wanted=True):
         same = jnp.logical_and(row == me_row, col == me_col)
         remote = pltpu.make_async_remote_copy(
             src_ref=src, dst_ref=dst, send_sem=send, recv_sem=recv,
             device_id={"row": row, "col": col}, device_id_type=MESH,
         )
 
-        @pl.when(jnp.logical_not(same))
+        @pl.when(jnp.logical_and(jnp.logical_not(same), wanted))
         def _():
             if begin:
                 remote.start()
@@ -109,21 +121,56 @@
                 pltpu.make_async_copy(src, dst, recv).start()
 
     def spread(begin):
-        def body(n, carry):
+        def rights(n, carry):
+            u = n // ncol
+            col = lax.rem(me_col + n, ncol)
+            m = slot(u)
+            for d in range(nh):
+                h = lax.rem(my_half + 1 + d, nh)
+                wanted = True
+                if nh == 2 and d == 0:
+                    wanted = jnp.logical_or(inner, u == 0)
+                move(owner(h, u), col, right_ref.at[col, u], rbuf.at[m, me_row, me_col],
+                     rsend.at[n * nh + d], rrecv.at[m, me_row], begin, wanted)
+            return carry
+
+        def lefts(n, carry):
             u = n // ncol
             col = lax.rem(me_col + n, ncol)
             m = slot(u)
             move(owner(my_half, u), col, left_ref.at[col, u], lbuf.at[m, me_row % per_half, me_col],
                  lsend.at[n], lrecv.at[m], begin)
-            for d in range(nh):
-                h = lax.rem(my_half + 1 + d, nh)
-                move(owner(h, u), col, right_ref.at[col, u], rbuf.at[m, me_row, me_col],
-                     rsend.at[n * nh + d], rrecv.at[m], begin)
-            return carry
-
-        lax.fori_loop(0, nu * ncol, body, 0)
+            return carry
+
+        lax.fori_loop(0, nu * ncol, rights, 0)
+        lax.fori_loop(0, nu * ncol, lefts, 0)
+
+    def take(m, row):
+        pltpu.make_async_copy(rbuf.at[m, row], rbuf.at[m, row], rrecv.at[m, row]).wait()
+
+    outer = my_half * (nrow - 1)
+    across = nrow - 1 - me_row
+
+    def relay(begin):
+        def body(m, carry):
+            copy = pltpu.make_async_remote_copy(
+                src_ref=rbuf.at[m, outer], dst_ref=rbuf.at[m, outer], send_sem=relays.at[m],
+                recv_sem=rrecv.at[m, outer], device_id={"row": across}, device_id_type=MESH,
+            )
+            if begin:
+                take(m, outer)
+                copy.start()
+            else:
+                copy.wait_send()
+            return carry
+
+        @pl.when(inner)
+        def _():
+            lax.fori_loop(0, slots, body, 0)
 
     spread(True)
+    if nh == 2:
+        relay(True)
 
     def give(m, begin):
         def body(n, carry):
@@ -149,7 +196,11 @@
 
     def work(m, carry):
         pltpu.make_async_copy(lbuf.at[m], lbuf.at[m], lrecv.at[m]).wait()
-        pltpu.make_async_copy(rbuf.at[m], rbuf.at[m], rrecv.at[m]).wait()
+        for row in range(nrow):
+            if nh == 2:
+                pl.when(jnp.logical_not(jnp.logical_and(inner, row == outer)))(functools.partial(take, m, row))
+            else:
+                take(m, row)
 
         def channel(c, carry):
             at = pl.multiple_of(c * depth, depth)
@@ -173,6 +224,8 @@
     lax.fori_loop(0, count, work, 0)
     pltpu.make_async_copy(out_ref, out_ref, crecv).wait()
     spread(False)
+    if nh == 2:
+        relay(False)
 
     def finish(m, carry):
         give(m, False)
@@ -185,6 +238,7 @@
     folds, depth, cols, width = out_ref.shape
     hidden = wo_ref.shape[0]
     block = 512
+    gain, bias = (jnp.broadcast_to(ref[...], (folds * cols, hidden)).T for ref in (gain_ref, bias_ref))
 
     def cast(n, carry):
         at = pl.multiple_of(n * block, block)
@@ -196,7 +250,7 @@
     def step(t, carry):
         x = scratch[pl.ds(t, hidden, stride=depth), :]
         x = x - jnp.mean(x, axis=0, keepdims=True)
-        x = x * lax.rsqrt(jnp.mean(x * x, axis=0, keepdims=True) + 1e-05) * gain_ref[...] + bias_ref[...]
+        x = x * lax.rsqrt(jnp.mean(x * x, axis=0, keepdims=True) + 1e-05) * gain + bias
         y = lax.dot_general(x.astype(jnp.bfloat16), wo_ref[...], TN, preferred_element_type=jnp.float32)
         y = (y * gate_ref[t]).astype(jnp.bfloat16)
         for p in range(folds):
@@ -216,25 +270,19 @@
     slots = nu - 1 if nh == 2 else 1
     per_half = nrow // nh
     rows = hidden // (ncol * nu) * depth
-    validity = mask.astype(jnp.float32)
-    row_valid = lax.dynamic_slice_in_dim(validity, lax.axis_index("row") * tile_rows, tile_rows)
-    col_valid = lax.dynamic_slice_in_dim(validity, lax.axis_index("col") * tile_cols, tile_cols)
-    cells = row_valid.reshape(folds, depth).T[:, :, None] * col_valid[None, None, :]
-    cells = cells.reshape(depth, lanes)
-    side_weights = jnp.concatenate([w_left, w_right], axis=1).T
     vmem = pl.BlockSpec(memory_space=pltpu.VMEM)
     anywhere = pl.BlockSpec(memory_space=pl.ANY)
     packed = jax.ShapeDtypeStruct((ncol, nu, rows, lanes), jnp.bfloat16)
     left, right, gate = pl.pallas_call(
         functools.partial(project, 4),
         out_shape=(packed, packed, jax.ShapeDtypeStruct((depth, lanes, width), jnp.float32)),
-        in_specs=[vmem] * 6,
+        in_specs=[vmem, pl.BlockSpec(memory_space=pltpu.SMEM)] + [vmem] * 6,
         out_specs=(vmem,) * 3,
         scratch_shapes=[pltpu.VMEM((2, hidden * depth, lanes), jnp.float32)],
         compiler_params=pltpu.CompilerParams(vmem_limit_bytes=LIMIT),
     )(
-        pair.reshape(folds, depth, tile_cols, width), cells,
-        ln_gain.reshape(1, width), ln_bias.reshape(1, width), side_weights, w_gate,
+        pair.reshape(folds, depth, tile_cols, width), mask, mask.reshape(ncol, tile_cols),
+        ln_gain.reshape(1, width), ln_bias.reshape(1, width), w_left, w_right, w_gate,
     )
     plane = pl.pallas_call(
         functools.partial(exchange, (nrow, ncol, nh, nu, depth)),
@@ -249,8 +297,9 @@
             pltpu.SemaphoreType.DMA((nu * ncol * nh,)),
             pltpu.SemaphoreType.DMA((slots * per_half * ncol,)),
             pltpu.SemaphoreType.DMA((slots,)),
+            pltpu.SemaphoreType.DMA((slots, nrow)),
+            pltpu.SemaphoreType.DMA,
             pltpu.SemaphoreType.DMA((slots,)),
-            pltpu.SemaphoreType.DMA,
         ],
         compiler_params=pltpu.CompilerParams(
             collective_id=0, has_side_effects=True, vmem_limit_bytes=LIMIT
@@ -265,8 +314,7 @@
         compiler_params=pltpu.CompilerParams(vmem_limit_bytes=LIMIT),
     )(
         plane.reshape(hidden * depth, lanes), gate,
-        jnp.broadcast_to(out_gain[:, None], (hidden, lanes)),
-        jnp.broadcast_to(out_bias[:, None], (hidden, lanes)), w_out,
+        out_gain.reshape(1, hidden), out_bias.reshape(1, hidden), w_out,
     )
     return out.reshape(tile_rows, tile_cols, width)
 

time: 101 us -> 84.4 us (0.84)
  Pallas kernels: 94.7 us -> 82.5 us
  local copies, waits for them, and re-layouts: 3.82 us -> 1.33 us
  other arithmetic: 1.94 us -> 0 us
    pallas_call x1, Pallas kernels: 76.1 us -> 63.8 us  [body(): pl.pallas_call(functools.partial(exchange, (nrow, ncol, nh, nu, depth)),...]
    unnamed x6 -> x0, local copies, waits for them, and re-layouts: 1.91 us -> none
    broadcast_in_dim x2 -> x0, local copies, waits for them, and re-layouts: 1.39 us -> none  [the longest x1 0.7 us: body(): jnp.broadcast_to(out_bias[:, None], (hidden, lanes))]
    reshape x1, local copies, waits for them, and re-layouts: 0.08 us -> 1.33 us  [body(): mask.reshape(ncol, tile_cols)]
where the time goes in v2:
time: 84.4 us; the launch traced here: 83.9 us
  Pallas kernels  82.5 us (98%)
  local copies, waits for them, and re-layouts  1.33 us (2%)
    pallas_call x1, Pallas kernels, body(): pl.pallas_call(functools.partial(exchange, (nrow, ncol, nh, nu, depth)),...  63.8 us
    pallas_call x1, Pallas kernels, body(): pl.pallas_call(functools.partial(project, 4), out_shape=(packed, packed,...  9.96 us
    pallas_call x1, Pallas kernels, body(): pl.pallas_call(output, out_shape=jax.ShapeDtypeStruct((folds, depth, tile...  8.82 us

profile of v2, /device:TPU:0, one launch (start us, length us, event | category | flops | bytes accessed | tf_op | source)
XLA Modules:
  0.0 83.9 jit_solution(365549807444702018)
XLA Ops:
  0.0 1.3 %reshape.25.cols_ref = s32[4,64]{1,0:T(4,128)} reshape(s32[256]{0:T(256)} %flag_ref.1) | data formatting | bytes 2048 | tf_op jit(solution)/shard_map/reshape | solution.py:284
  1.3 10.0 %shard_map.100 = (bf16[4,4,256,128]{3,2,1,0:T(8,128)(2,1)}, bf16[4,4,256,128]{3,2,1,0:T(8,128)(2,1)}, f32[32,128,128]{2,1,0:T(8,128)}) custom-call(bf16[2,32,64,128]{3,2,1,0:T(8,128)(2,1)} %bitcast.8, s32[256]{0:T(256)} %flag_ref.1, s32[4,64]{1,0:T(4,128)} %reshape.25.cols_ref, f32[1,128]{1,0:T(1,128)} %bitcast.9, f32[1,128]{1,0:T(1,128)} %bitcast.10, ...), custom_call_target="tpu_custom_call" | custom-call | tf_op jit(solution)/shard_map/pallas_call | solution.py:276
  11.3 63.8 %shard_map.101 = bf16[4,4,256,128]{3,2,1,0:T(8,128)(2,1)} custom-call(bf16[4,4,256,128]{3,2,1,0:T(8,128)(2,1)} %get-tuple-element.8.left_ref, bf16[4,4,256,128]{3,2,1,0:T(8,128)(2,1)} %get-tuple-element.9.right_ref), custom_call_target="tpu_custom_call" | custom-call | tf_op jit(solution)/shard_map/pallas_call | solution.py:287
  75.1 8.8 %shard_map.102 = bf16[2,32,64,128]{3,2,1,0:T(8,128)(2,1)} custom-call(bf16[4096,128]{1,0:T(8,128)(2,1)} %bitcast.7, f32[32,128,128]{2,1,0:T(8,128)} %get-tuple-element.10.gate_ref, f32[1,128]{1,0:T(1,128)} %bitcast.11, f32[1,128]{1,0:T(1,128)} %bitcast.12, bf16[128,128]{1,0:T(8,128)(2,1)} %wo_ref.1), custom_call_target="tpu_custom_call" | custom-call | tf_op jit(solution)/shard_map/pallas_call | solution.py:308

commit v3 on v2

--- a/solution.py
+++ b/solution.py
@@ -257,7 +257,7 @@
             out_ref[p, t] = y[p * cols : (p + 1) * cols]
         return carry
 
-    lax.fori_loop(0, depth, step, 0, unroll=2)
+    lax.fori_loop(0, depth, step, 0, unroll=4)
 
 
 def body(nrow, ncol, pair, mask, ln_gain, ln_bias, w_left, w_right, w_gate, w_out, out_gain, out_bias):
@@ -274,7 +274,7 @@
     anywhere = pl.BlockSpec(memory_space=pl.ANY)
     packed = jax.ShapeDtypeStruct((ncol, nu, rows, lanes), jnp.bfloat16)
     left, right, gate = pl.pallas_call(
-        functools.partial(project, 4),
+        functools.partial(project, 8),
         out_shape=(packed, packed, jax.ShapeDtypeStruct((depth, lanes, width), jnp.float32)),
         in_specs=[vmem, pl.BlockSpec(memory_space=pltpu.SMEM)] + [vmem] * 6,
         out_specs=(vmem,) * 3,

time: 84.4 us -> 81.9 us (0.970)
  Pallas kernels: 82.5 us -> 80 us
    pallas_call x1, Pallas kernels: 8.82 us -> 7.07 us  [body(): pl.pallas_call(output, out_shape=jax.ShapeDtypeStruct((folds, depth, tile...]
where the time goes in v3:
time: 81.9 us; the launch traced here: 81.4 us
  Pallas kernels  80 us (98%)
  local copies, waits for them, and re-layouts  1.33 us (2%)
    pallas_call x1, Pallas kernels, body(): pl.pallas_call(functools.partial(exchange, (nrow, ncol, nh, nu, depth)),...  63.8 us
    pallas_call x1, Pallas kernels, body(): pl.pallas_call(functools.partial(project, 8), out_shape=(packed, packed,...  9.19 us
    pallas_call x1, Pallas kernels, body(): pl.pallas_call(output, out_shape=jax.ShapeDtypeStruct((folds, depth, tile...  7.07 us

profile of v3, /device:TPU:0, one launch (start us, length us, event | category | flops | bytes accessed | tf_op | source)
XLA Modules:
  0.0 81.4 jit_solution(12243379233905514282)
XLA Ops:
  0.0 1.3 %reshape.25.cols_ref = s32[4,64]{1,0:T(4,128)} reshape(s32[256]{0:T(256)} %flag_ref.1) | data formatting | bytes 2048 | tf_op jit(solution)/shard_map/reshape | solution.py:284
  1.3 9.2 %shard_map.100 = (bf16[4,4,256,128]{3,2,1,0:T(8,128)(2,1)}, bf16[4,4,256,128]{3,2,1,0:T(8,128)(2,1)}, f32[32,128,128]{2,1,0:T(8,128)}) custom-call(bf16[2,32,64,128]{3,2,1,0:T(8,128)(2,1)} %bitcast.8, s32[256]{0:T(256)} %flag_ref.1, s32[4,64]{1,0:T(4,128)} %reshape.25.cols_ref, f32[1,128]{1,0:T(1,128)} %bitcast.9, f32[1,128]{1,0:T(1,128)} %bitcast.10, ...), custom_call_target="tpu_custom_call" | custom-call | tf_op jit(solution)/shard_map/pallas_call | solution.py:276
  10.5 63.8 %shard_map.101 = bf16[4,4,256,128]{3,2,1,0:T(8,128)(2,1)} custom-call(bf16[4,4,256,128]{3,2,1,0:T(8,128)(2,1)} %get-tuple-element.8.left_ref, bf16[4,4,256,128]{3,2,1,0:T(8,128)(2,1)} %get-tuple-element.9.right_ref), custom_call_target="tpu_custom_call" | custom-call | tf_op jit(solution)/shard_map/pallas_call | solution.py:287
  74.3 7.1 %shard_map.102 = bf16[2,32,64,128]{3,2,1,0:T(8,128)(2,1)} custom-call(bf16[4096,128]{1,0:T(8,128)(2,1)} %bitcast.7, f32[32,128,128]{2,1,0:T(8,128)} %get-tuple-element.10.gate_ref, f32[1,128]{1,0:T(1,128)} %bitcast.11, f32[1,128]{1,0:T(1,128)} %bitcast.12, bf16[128,128]{1,0:T(8,128)(2,1)} %wo_ref.1), custom_call_target="tpu_custom_call" | custom-call | tf_op jit(solution)/shard_map/pallas_call | solution.py:308
